TPU v7x, 128 devices: a whole 4x4x4 slice. The times are simulated.
128 devices in a mesh: seq: 16 (over x, z_hi, core), res: 8 (over y, z_lo).
Axes of the slice: x: 4, y: 4, z: 4 (z_hi: 2, z_lo: 2; z = z_hi * 2 + z_lo), core: 2. Of those that a mesh axis runs over, the one named last changes fastest.
Arguments:
- homolog_embedding: bfloat16 [512, 768, 256], P('seq', 'res'), may hold values from -6 to 6
- homolog_entry_flags: int32 [512, 768], P('seq', 'res'), may hold values 0 or 1
- amino_exists_flags: int32 [768], P('res'), may hold values 0 or 1
- couple_embedding: bfloat16 [768, 768, 128], P('res', 'seq'), may hold values from -6 to 6
- couple_layernorm_scale: float32 [128], replicated, may hold values from 0.1 to 1.9
- couple_offset_matrix: bfloat16 [128, 8], replicated, may hold values from -0.5 to 0.5
- horizontal_layernorm_scale: float32 [256], replicated, may hold values from 0.1 to 1.9
- horizontal_qkvg_matrix: bfloat16 [4, 256, 256], replicated, may hold values from -9 to 9
- horizontal_final_matrix: bfloat16 [256, 256], replicated, may hold values from -4 to 4
- vertical_layernorm_scale: float32 [256], replicated, may hold values from 0.1 to 1.9
- vertical_qkvg_matrix: bfloat16 [4, 256, 256], replicated, may hold values from -9 to 9
- vertical_final_matrix: bfloat16 [256, 256], replicated, may hold values from -4 to 4
Outputs:
- horizontal_increment: bfloat16 [512, 768, 256], P('seq', 'res')
- col_update: bfloat16 [512, 768, 256], P('seq', 'res')
All inputs are finite; a program needn't handle non-finite values. No bound on the sum of `homolog_entry_flags` or of `amino_exists_flags` on one device may be relied on, other than what follows from the above.
Results may differ from a plain program's by a relative error of at most 0.02.
The roundings to bfloat16 on the way count: a program that leaves them out, or rounds other values in their place, can miss the bound.
Values may be sent and summed in bfloat16 or wider, within the bound.
A program may use at most 128 MiB of HBM per device.

v0:
```python
import jax
import jax.numpy as jnp
from jax import lax
from jax.sharding import PartitionSpec as P


def normalize(inputs, gain_vec):
    floats = inputs.astype(jnp.float32)
    centre = jnp.mean(floats, axis=-1, keepdims=True)
    spread = jnp.mean(jnp.square(floats - centre), axis=-1, keepdims=True)
    return ((floats - centre) * lax.rsqrt(spread + 1e-05) * gain_vec).astype(jnp.bfloat16)


def attend(projected, key_present, pair_bias):
    head_dim = projected.shape[-1]
    asking_vectors = projected[:, :, 0]
    key_rows = projected[:, :, 1]
    values = projected[:, :, 2]
    gate_logit = projected[:, :, 3]
    scores = jnp.einsum(
        "ihd,jhd->hij", asking_vectors, key_rows, preferred_element_type=jnp.float32
    ) * head_dim ** (-0.5)
    scores = scores + (key_present.astype(jnp.float32) - 1.0)[None, None, :] * 1000000000.0
    if pair_bias is not None:
        scores = scores + pair_bias.astype(jnp.float32)
    peak = jnp.max(scores, axis=-1, keepdims=True)
    powers = jnp.exp(scores - peak)
    totals = jnp.sum(powers, axis=-1)
    mixture = jnp.einsum(
        "hij,jhd->ihd", powers.astype(jnp.bfloat16), values, preferred_element_type=jnp.float32
    )
    mixture = mixture / jnp.transpose(totals)[:, :, None]
    return (jax.nn.sigmoid(gate_logit.astype(jnp.float32)) * mixture).astype(jnp.bfloat16)


def per_device(
    homolog_embedding,
    homolog_entry_flags,
    amino_exists_flags,
    couple_embedding,
    couple_layernorm_scale,
    couple_offset_matrix,
    horizontal_layernorm_scale,
    horizontal_qkvg_matrix,
    horizontal_final_matrix,
    vertical_layernorm_scale,
    vertical_qkvg_matrix,
    vertical_final_matrix,
):
    homolog_lines, amino_positions, feature_depth = homolog_embedding.shape
    num_heads = couple_offset_matrix.shape[1]
    head_dim = feature_depth // num_heads
    res_count = lax.axis_size("res")
    seq_count = lax.axis_size("seq")
    all_res = amino_positions * res_count
    all_seq = homolog_lines * seq_count
    per_group = amino_positions // seq_count
    vertical_probabilities = vertical_qkvg_matrix.reshape(4, feature_depth, num_heads, head_dim)
    mask_float = homolog_entry_flags.astype(jnp.bfloat16)
    pair_norm = normalize(couple_embedding, couple_layernorm_scale)
    bias_tile = jnp.einsum(
        "ijc,ch->hij", pair_norm, couple_offset_matrix, preferred_element_type=jnp.float32
    ).astype(jnp.bfloat16)
    key_present = (homolog_entry_flags * amino_exists_flags[None, :]).astype(jnp.bfloat16)
    horizontal_probabilities = horizontal_qkvg_matrix.reshape(4, feature_depth, num_heads, head_dim)
    col_update = None
    local_seqs = homolog_lines // res_count
    arrived, live_rows, mask_rows = (
        lax.all_to_all(homolog_embedding, "res", split_axis=0, concat_axis=1, tiled=True),
        lax.all_to_all(key_present, "res", split_axis=0, concat_axis=1, tiled=True),
        lax.all_to_all(mask_float, "res", split_axis=0, concat_axis=1, tiled=True),
    )
    stacked = lax.all_gather(bias_tile[None], ("seq", "res"), axis=0, tiled=True)
    pair_cols = bias_tile.shape[2]
    stacked = stacked.reshape(seq_count, res_count, num_heads, amino_positions, pair_cols)
    pair_bias = jnp.transpose(stacked, (2, 1, 3, 0, 4)).reshape(
        num_heads, all_res, seq_count * pair_cols
    )
    normed = normalize(arrived, horizontal_layernorm_scale)
    projected = jnp.einsum(
        "src,achd->srhad", normed, horizontal_probabilities, preferred_element_type=jnp.float32
    ).astype(jnp.bfloat16)
    sigmoid_scaled = lax.map(
        lambda element: attend(element[0], element[1], pair_bias), (projected, live_rows)
    )
    row_delta = jnp.dot(
        sigmoid_scaled.reshape(local_seqs, all_res, feature_depth),
        horizontal_final_matrix,
        preferred_element_type=jnp.float32,
    ).astype(jnp.bfloat16)
    horizontal_increment = lax.all_to_all(row_delta, "res", split_axis=1, concat_axis=0, tiled=True)
    vertical_source = (
        homolog_embedding.astype(jnp.float32) + horizontal_increment.astype(jnp.float32)
    ).astype(jnp.bfloat16)
    grouped = vertical_source.reshape(homolog_lines, seq_count, per_group, feature_depth)
    grouped_live = mask_float.reshape(homolog_lines, seq_count, per_group)
    columns = lax.all_to_all(grouped, "seq", split_axis=1, concat_axis=0, tiled=True)
    col_live = lax.all_to_all(grouped_live, "seq", split_axis=1, concat_axis=0, tiled=True)
    count = columns.shape[2]
    normed = normalize(columns[:, 0], vertical_layernorm_scale)
    projected = jnp.einsum(
        "sjc,achd->jshad", normed, vertical_probabilities, preferred_element_type=jnp.float32
    ).astype(jnp.bfloat16)
    sigmoid_scaled = lax.map(
        lambda element: attend(element[0], element[1], None),
        (projected, jnp.transpose(col_live[:, 0])),
    )
    col_delta = jnp.dot(
        sigmoid_scaled.reshape(count, all_seq, feature_depth),
        vertical_final_matrix,
        preferred_element_type=jnp.float32,
    ).astype(jnp.bfloat16)
    col_delta = jnp.transpose(col_delta, (1, 0, 2))[:, None]
    col_update = lax.all_to_all(col_delta, "seq", split_axis=0, concat_axis=1, tiled=True)
    col_update = col_update.reshape(homolog_lines, amino_positions, feature_depth)
    return (horizontal_increment, col_update)


def solution(mesh):
    in_specs = (
        P("seq", "res", None),
        P("seq", "res"),
        P("res"),
        P("res", "seq", None),
        P(),
        P(),
        P(),
        P(),
        P(),
        P(),
        P(),
        P(),
    )
    out_specs = (P("seq", "res", None), P("seq", "res", None))
    return jax.shard_map(
        per_device, mesh=mesh, in_specs=in_specs, out_specs=out_specs, check_vma=False
    )
```

profile of v0, /device:TPU:1, one launch (start us, length us, event | category | flops | bytes accessed | tf_op | source)
XLA Modules:
  0.0 718.8 jit_solution(16986360274550149826)
XLA Ops:
  7.3 2.0 convert_reduce_fusion
  9.3 2.5 fusion.64
  11.9 2.8 fusion.76
  14.7 11.3 %all_to_all.85 = bf16[8,4,96]{2,1,0:T(4,128)(2,1)S(1)} all-to-all(bf16[8,4,96]{2,1,0:T(4,128)(2,1)S(1)} %bitcast.238), channel_id=1, replica_groups=mesh['seq'=16,'res'=8] {'res'}, dimensions={0} | all-to-all | bytes 12288 | tf_op jit(solution)/shard_map/all_to_all | solution.py:70
  26.0 3.6 all-to-all-start
  30.0 24.0 %all-to-all-done = bf16[32,96,256]{2,1,0:T(8,128)(2,1)S(1)} async-done(((bf16[32,96,256]{2,1,0:T(8,128)(2,1)}), bf16[32,96,256]{2,1,0:T(8,128)(2,1)S(1)}, u32[]{:S(2)}, u32[]{:S(2)}) %all-to-all-start) | async-done | bytes 1572896 | tf_op jit(solution)/shard_map/all_to_all | solution.py:69
  56.9 4.5 convert_bitcast_fusion.1
  61.4 303.6 %all-gather.3.cloned.1.call-done = bf16[1024,96,48]{2,0,1:T(8,128)(2,1)} async-done(((bf16[8,96,48]{2,0,1:T(8,128)(2,1)}), bf16[1024,96,48]{2,0,1:T(8,128)(2,1)}) %all-gather.3.cloned.1.call-update) | async-done | bytes 9437200 | tf_op jit(solution)/shard_map/all_gather | solution.py:73
  365.0 35.8 %copy.81 = bf16[8,8,96,16,48]{2,1,4,3,0:T(8,128)(2,1)} copy(bf16[8,8,96,16,48]{4,0,1,3,2:T(8,128)(2,1)} %bitcast.216) | data formatting | bytes 18874368 | tf_op jit(solution)/shard_map/transpose | solution.py:76
  400.8 20.3 %reshape.155 = bf16[8,768,768]{1,2,0:T(8,128)(2,1)} reshape(bf16[8,8,96,16,48]{2,1,4,3,0:T(8,128)(2,1)} %copy.81) | data formatting | bytes 18874368 | tf_op jit(solution)/shard_map/reshape | solution.py:76
  421.1 124.2 %while.24 = (s32[]{:T(128)}, bf16[4,768,8,32]{1,3,2,0:T(8,128)(2,1)S(1)}, bf16[4,768,8,4,32]{1,4,2,3,0:T(8,128)(2,1)}, bf16[4,768]{1,0:T(4,128)(2,1)S(1)}, bf16[8,768,768]{1,2,0:T(8,128)(2,1)}, /*index=5*/s32[]{:T(128)}) while((s32[]{:T(128)}, bf16[4,768,8,32]{1,3,2,0:T(8,128)(2,1)S(1)}, bf16[4,768,8,4,32]{1,4,2,3,0:T(8,128)(2,1)}, ...), condition=%wide.region_7.8_spmd, body=%wide.region_4.7_spmd.sunk | while | flops 647813376 | bytes 71303768 | solution.py:83
  422.7 11.1 %fusion.99 = (f32[8,768]{1,0:T(8,128)S(1)}, f32[8,768,768]{1,2,0:T(8,128)}) fusion(bf16[8,768,768]{1,2,0:T(8,128)(2,1)} %get-tuple-element.234, f32[768]{0:T(1024)S(1)} %multiply_reduce_fusion.2, bf16[768,8,4,32]{0,3,1,2:T(8,128)(2,1)S(1)} %dynamic-slice_bitcast_fusion.4), kind=kOutput, calls=%fused_computation.82.clone.1 | convolution fusion | flops 325576704 | bytes 29126656 | tf_op jit(solution)/shard_map/while/body/eval_jaxpr/ihd,jhd->hij/dot_general | solution.py:20
  433.8 8.9 %fusion.100 = f32[8,768]{1,0:T(8,128)S(1)} fusion(f32[8,768,768]{1,2,0:T(8,128)} %get-tuple-element.210, f32[8,768]{1,0:T(8,128)S(1)} %get-tuple-element.211), kind=kLoop, calls=%fused_computation.21.clone.1 | loop fusion | flops 9431040 | bytes 18923520 | tf_op jit(solution)/shard_map/while/body/eval_jaxpr/reduce_sum | solution.py:28
  442.6 9.5 %fusion.101 = bf16[4,768,8,32]{1,3,2,0:T(8,128)(2,1)S(1)} fusion(bf16[4,768,8,32]{1,3,2,0:T(8,128)(2,1)S(1)} %get-tuple-element.225, s32[]{:T(128)S(6)} %copy.109, f32[8,768,768]{1,2,0:T(8,128)} %get-tuple-element.210, f32[8,768]{1,0:T(8,128)S(1)} %get-tuple-element.211, bf16[768,8,4,32]{0,3,1,2:T(8,128)(2,1)S(1)} %dynamic-slice_bitcast_fusion.4, ...), kind=kOutput, calls=%fused_computation.31.clone.1 | convolution fusion | flops 312803328 | bytes 20103172 | tf_op jit(solution)/shard_map/while/body/eval_jaxpr/hij,jhd->ihd/dot_general | solution.py:29
  453.7 11.1 %fusion.99 = (f32[8,768]{1,0:T(8,128)S(1)}, f32[8,768,768]{1,2,0:T(8,128)}) fusion(bf16[8,768,768]{1,2,0:T(8,128)(2,1)} %get-tuple-element.234, f32[768]{0:T(1024)S(1)} %multiply_reduce_fusion.2, bf16[768,8,4,32]{0,3,1,2:T(8,128)(2,1)S(1)} %dynamic-slice_bitcast_fusion.4), kind=kOutput, calls=%fused_computation.82.clone.1 | convolution fusion | flops 325576704 | bytes 29126656 | tf_op jit(solution)/shard_map/while/body/eval_jaxpr/ihd,jhd->hij/dot_general | solution.py:20
  464.8 8.9 %fusion.100 = f32[8,768]{1,0:T(8,128)S(1)} fusion(f32[8,768,768]{1,2,0:T(8,128)} %get-tuple-element.210, f32[8,768]{1,0:T(8,128)S(1)} %get-tuple-element.211), kind=kLoop, calls=%fused_computation.21.clone.1 | loop fusion | flops 9431040 | bytes 18923520 | tf_op jit(solution)/shard_map/while/body/eval_jaxpr/reduce_sum | solution.py:28
  473.7 9.5 %fusion.101 = bf16[4,768,8,32]{1,3,2,0:T(8,128)(2,1)S(1)} fusion(bf16[4,768,8,32]{1,3,2,0:T(8,128)(2,1)S(1)} %get-tuple-element.225, s32[]{:T(128)S(6)} %copy.109, f32[8,768,768]{1,2,0:T(8,128)} %get-tuple-element.210, f32[8,768]{1,0:T(8,128)S(1)} %get-tuple-element.211, bf16[768,8,4,32]{0,3,1,2:T(8,128)(2,1)S(1)} %dynamic-slice_bitcast_fusion.4, ...), kind=kOutput, calls=%fused_computation.31.clone.1 | convolution fusion | flops 312803328 | bytes 20103172 | tf_op jit(solution)/shard_map/while/body/eval_jaxpr/hij,jhd->ihd/dot_general | solution.py:29
  484.7 11.1 %fusion.99 = (f32[8,768]{1,0:T(8,128)S(1)}, f32[8,768,768]{1,2,0:T(8,128)}) fusion(bf16[8,768,768]{1,2,0:T(8,128)(2,1)} %get-tuple-element.234, f32[768]{0:T(1024)S(1)} %multiply_reduce_fusion.2, bf16[768,8,4,32]{0,3,1,2:T(8,128)(2,1)S(1)} %dynamic-slice_bitcast_fusion.4), kind=kOutput, calls=%fused_computation.82.clone.1 | convolution fusion | flops 325576704 | bytes 29126656 | tf_op jit(solution)/shard_map/while/body/eval_jaxpr/ihd,jhd->hij/dot_general | solution.py:20
  495.9 8.9 %fusion.100 = f32[8,768]{1,0:T(8,128)S(1)} fusion(f32[8,768,768]{1,2,0:T(8,128)} %get-tuple-element.210, f32[8,768]{1,0:T(8,128)S(1)} %get-tuple-element.211), kind=kLoop, calls=%fused_computation.21.clone.1 | loop fusion | flops 9431040 | bytes 18923520 | tf_op jit(solution)/shard_map/while/body/eval_jaxpr/reduce_sum | solution.py:28
  504.7 9.5 %fusion.101 = bf16[4,768,8,32]{1,3,2,0:T(8,128)(2,1)S(1)} fusion(bf16[4,768,8,32]{1,3,2,0:T(8,128)(2,1)S(1)} %get-tuple-element.225, s32[]{:T(128)S(6)} %copy.109, f32[8,768,768]{1,2,0:T(8,128)} %get-tuple-element.210, f32[8,768]{1,0:T(8,128)S(1)} %get-tuple-element.211, bf16[768,8,4,32]{0,3,1,2:T(8,128)(2,1)S(1)} %dynamic-slice_bitcast_fusion.4, ...), kind=kOutput, calls=%fused_computation.31.clone.1 | convolution fusion | flops 312803328 | bytes 20103172 | tf_op jit(solution)/shard_map/while/body/eval_jaxpr/hij,jhd->ihd/dot_general | solution.py:29
  515.8 11.1 %fusion.99 = (f32[8,768]{1,0:T(8,128)S(1)}, f32[8,768,768]{1,2,0:T(8,128)}) fusion(bf16[8,768,768]{1,2,0:T(8,128)(2,1)} %get-tuple-element.234, f32[768]{0:T(1024)S(1)} %multiply_reduce_fusion.2, bf16[768,8,4,32]{0,3,1,2:T(8,128)(2,1)S(1)} %dynamic-slice_bitcast_fusion.4), kind=kOutput, calls=%fused_computation.82.clone.1 | convolution fusion | flops 325576704 | bytes 29126656 | tf_op jit(solution)/shard_map/while/body/eval_jaxpr/ihd,jhd->hij/dot_general | solution.py:20
  526.9 8.9 %fusion.100 = f32[8,768]{1,0:T(8,128)S(1)} fusion(f32[8,768,768]{1,2,0:T(8,128)} %get-tuple-element.210, f32[8,768]{1,0:T(8,128)S(1)} %get-tuple-element.211), kind=kLoop, calls=%fused_computation.21.clone.1 | loop fusion | flops 9431040 | bytes 18923520 | tf_op jit(solution)/shard_map/while/body/eval_jaxpr/reduce_sum | solution.py:28
  535.8 9.5 %fusion.101 = bf16[4,768,8,32]{1,3,2,0:T(8,128)(2,1)S(1)} fusion(bf16[4,768,8,32]{1,3,2,0:T(8,128)(2,1)S(1)} %get-tuple-element.225, s32[]{:T(128)S(6)} %copy.109, f32[8,768,768]{1,2,0:T(8,128)} %get-tuple-element.210, f32[8,768]{1,0:T(8,128)S(1)} %get-tuple-element.211, bf16[768,8,4,32]{0,3,1,2:T(8,128)(2,1)S(1)} %dynamic-slice_bitcast_fusion.4, ...), kind=kOutput, calls=%fused_computation.31.clone.1 | convolution fusion | flops 312803328 | bytes 20103172 | tf_op jit(solution)/shard_map/while/body/eval_jaxpr/hij,jhd->ihd/dot_general | solution.py:29
  545.9 2.4 copy.83
  548.3 3.6 all-to-all-start.2
  552.6 23.3 %all-to-all-done.2 = bf16[4,768,256]{2,0,1:T(4,128)(2,1)S(1)} async-done(((bf16[4,768,256]{2,0,1:T(4,128)(2,1)}), bf16[4,768,256]{2,0,1:T(4,128)(2,1)S(1)}, u32[]{:S(2)}, u32[]{:S(2)}) %all-to-all-start.2) | async-done | bytes 1572896 | tf_op jit(solution)/shard_map/all_to_all | solution.py:91
  575.9 6.7 all-to-all-start.4
  582.6 2.0 copy.104
  584.6 2.4 all_to_all.71
  587.0 3.6 add_convert_fusion
  590.6 7.4 %all-to-all-start.3 = ((bf16[32,16,6,256]{3,0,2,1:T(8,128)(2,1)}), bf16[32,16,6,256]{3,0,2,1:T(8,128)(2,1)S(1)}, u32[]{:S(2)}, u32[]{:S(2)}) async-start(bf16[32,16,6,256]{3,0,2,1:T(8,128)(2,1)} %bitcast.225), calls=%async_computation.3 | async-start | bytes 3145728 | tf_op jit(solution)/shard_map/all_to_all | solution.py:97
  598.0 2.0 copy.87
  600.2 20.7 %all-to-all-done.3 = bf16[32,16,6,256]{3,0,2,1:T(8,128)(2,1)S(1)} async-done(((bf16[32,16,6,256]{3,0,2,1:T(8,128)(2,1)}), bf16[32,16,6,256]{3,0,2,1:T(8,128)(2,1)S(1)}, u32[]{:S(2)}, u32[]{:S(2)}) %all-to-all-start.3) | async-done | bytes 1572896 | tf_op jit(solution)/shard_map/all_to_all | solution.py:97
  624.4 4.5 convert_bitcast_fusion
  628.9 42.5 %while.25 = (s32[]{:T(128)}, bf16[6,512,8,32]{1,3,2,0:T(8,128)(2,1)S(1)}, bf16[6,512,8,4,32]{1,4,2,3,0:T(8,128)(2,1)}, bf16[6,512]{1,0:T(8,128)(2,1)S(1)}, s32[]{:T(128)}) while((s32[]{:T(128)}, bf16[6,512,8,32]{1,3,2,0:T(8,128)(2,1)S(1)}, bf16[6,512,8,4,32]{1,4,2,3,0:T(8,128)(2,1)}, bf16[6,512]{1,0:T(8,128)(2,1)S(1)}, s32[]{:T(128)}) %tuple.72), condition=%wide.region_13.14_spmd, body=%wide.region_10.13_spmd.sunk | while | flops 292414976 | bytes 28664912 | solution.py:104
  632.1 1.9 fusion.104
  639.2 1.9 fusion.104
  644.4 1.9 fusion.103
  646.3 1.9 fusion.104
  653.4 1.9 fusion.104
  660.4 1.9 fusion.104
  667.5 1.9 fusion.104
  672.0 2.2 copy.91
  674.2 5.0 all-to-all-start.5
  679.2 2.0 copy.94
  681.3 26.6 %all-to-all-done.5 = bf16[512,1,6,256]{3,2,1,0:T(8,128)(2,1)} async-done(((bf16[512,1,6,256]{3,2,1,0:T(8,128)(2,1)}), bf16[512,1,6,256]{3,2,1,0:T(8,128)(2,1)}, u32[]{:S(2)}, u32[]{:S(2)}) %all-to-all-start.5) | async-done | bytes 1572896 | tf_op jit(solution)/shard_map/all_to_all | solution.py:114
  707.9 1.9 copy.92
  709.9 2.0 copy.95
  (87 shorter events, 43.9 us)
Async XLA Ops:
  7.2 538.1 %copy-start = (bf16[256,256]{1,0:T(8,128)(2,1)S(1)}, bf16[256,256]{1,0:T(8,128)(2,1)}, u32[]{:S(2)}) copy-start(bf16[256,256]{1,0:T(8,128)(2,1)} %param.24) | copy-start | bytes 393220
  7.2 4.7 copy-start.1
  7.2 4.7 copy-start.11
  7.2 4.7 copy-start.12
  7.2 357.8 %all-gather.3.cloned.1.call-start = ((), (), s32[]{:S(2)}) async-start(), calls=%async_computation.6 | async-start | bytes 25362432 | tf_op jit(solution)/shard_map/all_gather | solution.py:73
  9.3 5.4 copy-start.7
  9.3 5.4 copy-start.10
  14.6 15.0 %copy-start.5 = (bf16[4,256,256]{2,1,0:T(8,128)(2,1)S(1)}, bf16[4,256,256]{2,1,0:T(8,128)(2,1)}, u32[]{:S(2)}) copy-start(bf16[4,256,256]{2,1,0:T(8,128)(2,1)} %param.23) | copy-start | bytes 1572868
  26.0 28.0 %all-to-all-start = ((bf16[32,96,256]{2,1,0:T(8,128)(2,1)}), bf16[32,96,256]{2,1,0:T(8,128)(2,1)S(1)}, u32[]{:S(2)}, u32[]{:S(2)}) async-start(bf16[32,96,256]{2,1,0:T(8,128)(2,1)} %param.16), calls=%async_computation | async-start | bytes 3145728 | tf_op jit(solution)/shard_map/all_to_all | solution.py:69
  29.6 26.1 %copy-start.8 = (f32[256]{0:T(256)S(1)}, f32[256]{0:T(256)}, u32[]{:S(2)}) copy-start(f32[256]{0:T(256)} %param.22) | copy-start | bytes 3076
  400.8 20.4 %copy-start.3 = (bf16[4,768,8,32]{1,3,2,0:T(8,128)(2,1)S(1)}, bf16[4,768,8,32]{1,3,2,0:T(8,128)(2,1)}, u32[]{:S(2)}) copy-start(bf16[4,768,8,32]{1,3,2,0:T(8,128)(2,1)} %custom-call) | copy-start | bytes 4718596
  548.3 27.6 %all-to-all-start.2 = ((bf16[4,768,256]{2,0,1:T(4,128)(2,1)}), bf16[4,768,256]{2,0,1:T(4,128)(2,1)S(1)}, u32[]{:S(2)}, u32[]{:S(2)}) async-start(bf16[4,768,256]{2,0,1:T(4,128)(2,1)} %copy.83), calls=%async_computation.2 | async-start | bytes 3145728 | tf_op jit(solution)/shard_map/all_to_all | solution.py:91
  575.9 14.7 %all-to-all-start.4 = ((bf16[32,16,6]{0,2,1:T(8,128)(2,1)}), bf16[32,16,6]{0,2,1:T(8,128)(2,1)S(1)}, u32[]{:S(2)}, u32[]{:S(2)}) async-start(bf16[32,16,6]{0,2,1:T(8,128)(2,1)} %reshape.159), calls=%async_computation.4 | async-start | bytes 65536 | tf_op jit(solution)/shard_map/all_to_all | solution.py:98
  590.6 30.3 %all-to-all-start.3 = ((bf16[32,16,6,256]{3,0,2,1:T(8,128)(2,1)}), bf16[32,16,6,256]{3,0,2,1:T(8,128)(2,1)S(1)}, u32[]{:S(2)}, u32[]{:S(2)}) async-start(bf16[32,16,6,256]{3,0,2,1:T(8,128)(2,1)} %bitcast.225), calls=%async_computation.3 | async-start | bytes 3145728 | tf_op jit(solution)/shard_map/all_to_all | solution.py:97
  598.0 24.3 %copy-start.9 = (f32[256]{0:T(256)S(1)}, f32[256]{0:T(256)}, u32[]{:S(2)}) copy-start(f32[256]{0:T(256)} %param.25) | copy-start | bytes 3076
  623.3 1.0 copy-start.2
  624.4 4.5 copy-start.4
  628.9 42.5 %copy-start.6 = (bf16[256,256]{1,0:T(8,128)(2,1)S(1)}, bf16[256,256]{1,0:T(8,128)(2,1)}, u32[]{:S(2)}) copy-start(bf16[256,256]{1,0:T(8,128)(2,1)} %param.27) | copy-start | bytes 393220
  674.2 33.7 %all-to-all-start.5 = ((bf16[512,1,6,256]{3,2,1,0:T(8,128)(2,1)}), bf16[512,1,6,256]{3,2,1,0:T(8,128)(2,1)}, u32[]{:S(2)}, u32[]{:S(2)}) async-start(bf16[512,1,6,256]{3,2,1,0:T(8,128)(2,1)} %copy.91), calls=%async_computation.5 | async-start | bytes 4194304 | tf_op jit(solution)/shard_map/all_to_all | solution.py:114
Sparse Core Ops, SparseCore 0:
  14.8 350.1 all-gather.2
where the time goes:
time: 721 us; the launch traced here: 719 us
  waiting for transfers between devices  398 us (55%)
  matrix products  118 us (16%)
  local copies, waits for them, and re-layouts  89.5 us (12%)
  other arithmetic  60.5 us (8%)
  starting transfers between devices  26.3 us (4%)
  between operations  14.4 us (2%)
  blocking collectives  11.3 us (2%)
    all_gather x1, waiting for transfers between devices, per_device(): lax.all_gather(bias_tile[None], ('seq', 'res'), axis=0, tiled=True)  304 us
    dot_general x10, matrix products, attend(): jnp.einsum('ihd,jhd->hij', asking_vectors, key_rows, preferred_element_ty...  55.9 us
    dot_general x10, matrix products, attend(): jnp.einsum('hij,jhd->ihd', powers.astype(jnp.bfloat16), values, preferred...  49.3 us
    reduce_sum x10, other arithmetic, attend(): totals = jnp.sum(powers, axis=-1)  47 us
    transpose x1, local copies, waits for them, and re-layouts, per_device(): jnp.transpose(stacked, (2, 1, 3, 0, 4))  35.8 us
    all_to_all x1, waiting for transfers between devices, per_device(): lax.all_to_all(col_delta, 'seq', split_axis=0, concat_axis=1, tiled=True)  26.6 us
    all_to_all x1, waiting for transfers between devices, per_device(): lax.all_to_all(homolog_embedding, 'res', split_axis=0, concat_axis=1, til...  24 us
    all_to_all x1, waiting for transfers between devices, per_device(): lax.all_to_all(row_delta, 'res', split_axis=1, concat_axis=0, tiled=True)  23.3 us
  transfers between devices with their start and end apart: 6, of which 5 were waited for; matrix products, arithmetic and copies ran while one was open for 3% of the time, Pallas kernels for 0%

commit v1 on v0

v1 whole, which is shorter than its diff:
```python
import jax
import jax.numpy as jnp
from jax import lax
from jax.experimental import pallas as pl
from jax.experimental.pallas import tpu as pltpu
from jax.sharding import PartitionSpec as P

F32 = jnp.float32
BF = jnp.bfloat16
MESH = pl.DeviceIdType.MESH
HEADS = 8
WIDTH = 32
CHAN = 256
QROWS = 64
LOG2E = 1.4426950408889634
VLIM = 63 * 2**20


def nt(a, b):
    return lax.dot_general(a, b, (((1,), (1,)), ((), ())), preferred_element_type=F32)


def tn(a, b):
    return lax.dot_general(a, b, (((0,), (0,)), ((), ())), preferred_element_type=F32)


def nn(a, b):
    return lax.dot_general(a, b, (((1,), (0,)), ((), ())), preferred_element_type=F32)


def norm(x, gain):
    f = x.astype(F32)
    c = f - jnp.mean(f, axis=-1, keepdims=True)
    v = jnp.mean(c * c, axis=-1, keepdims=True)
    return (c * lax.rsqrt(v + 1e-5) * gain).astype(BF)


def peak_of(a):
    n = a.shape[0]
    while n > 8 and n % 16 == 0:
        n //= 2
        a = jnp.maximum(a[:n], a[n:])
    top = a[:8]
    for i in range(8, n, 8):
        top = jnp.maximum(top, a[i:i + 8])
    return jnp.max(top, axis=0, keepdims=True)


def project(x, gain, col, wk_ref, wt_ref, keys, asks, pick_asks, xn_s, k_s, q_s, v_s, g_s):
    xn = norm(x, gain)
    xn_s[...] = xn
    lane = lax.broadcasted_iota(jnp.int32, (x.shape[0], 128), 1)
    add = jnp.where(lane == WIDTH, col, 0.0)
    add = jnp.concatenate([add, add], axis=1)
    for h in range(0, HEADS, 2):
        at = slice(h * 128, (h + 2) * 128)
        key = (nn(xn, wk_ref[:, at]) + add).astype(BF)
        for lo, n, to in keys:
            k_s[pl.ds(to, n), at] = key[lo:lo + n]
    vt = nt(wt_ref[1], xn).astype(BF)
    for lo, n, to in keys:
        for h in range(HEADS):
            v_s[h, :WIDTH, pl.ds(to, n)] = vt[h * WIDTH:(h + 1) * WIDTH, lo:lo + n]
    xq = pick_asks(xn_s)
    qt = (nt(wt_ref[0], xq) * (WIDTH ** -0.5 * LOG2E)).astype(BF)
    gt = nt(wt_ref[2], xq).astype(BF)
    for lo, n, to in asks:
        g_s[:, pl.ds(to, n)] = gt[:, lo:lo + n]
        for h in range(HEADS):
            q_s[h, :WIDTH, pl.ds(to, n)] = qt[h * WIDTH:(h + 1) * WIDTH, lo:lo + n]


def attend(klo, nk, qlo, nq, bias_ref, k_s, q_s, v_s, g_s, o_s):
    keys, cols = pl.ds(klo, nk), pl.ds(qlo, nq)

    def score(h):
        sc = nn(k_s[keys, h * 128:h * 128 + QROWS], q_s[h, :, cols])
        return sc if bias_ref is None else sc + bias_ref[h]

    sc = score(0)
    for h in range(HEADS):
        ahead = score(h + 1) if h + 1 < HEADS else None
        p = jnp.exp2(sc - peak_of(sc)).astype(BF)
        o = nn(v_s[h, :, keys], p)
        at = slice(h * WIDTH, (h + 1) * WIDTH)
        gate = jax.nn.sigmoid(g_s[at, cols].astype(F32))
        o_s[at, cols] = (gate * (o[:WIDTH] * (1.0 / o[WIDTH:WIDTH + 1]))).astype(BF)
        sc = ahead


def pick(table, which):
    at = lax.broadcasted_iota(jnp.int32, table.shape, 1) == which
    return jnp.sum(jnp.where(at, table, 0.0), axis=1, keepdims=True)


def kernel(pair_hbm, pgain_ref, pw_ref, own_hbm, flags_ref, amino_ref, rgain_ref, rw_hbm, ro_ref, cgain_ref, cw_hbm, co_ref,
           inc_hbm, fin_hbm,
           pair_ref, own_ref, rw_ref, cw_ref, inc_ref, perm_s, buf, bias_s, turn_s, rsend_ref, csend_ref, rows_s, rmask_s, cmask_s, col_s, out_s, done_s, ctab_s, xn_s,
           k_s, q_s, v_s, g_s, o_s, wk_s, wt_s,
           gsend, grecv, psend, precv, ysend, yrecv, zsend, zrecv, bsend, brecv, csend, crecv, esend, erecv,
           rmsend, rmrecv, cmsend, cmrecv, lsem, tsem):
    s_me = lax.axis_index("seq")
    r_me = lax.axis_index("res")
    x, zhi, c = s_me // 4, (s_me // 2) % 2, s_me % 2
    y, zlo = r_me // 2, r_me % 2

    def along_x(d):
        return ((x + d) % 4 * 4 + zhi * 2 + c, r_me)

    def along_y(d):
        return (s_me, (y + d) % 4 * 2 + zlo)

    far = (x * 4 + (1 - zhi) * 2 + c, r_me)
    near = (s_me, y * 2 + 1 - zlo)
    twin = (x * 4 + zhi * 2 + 1 - c, r_me)

    def res_peer(k):
        return (s_me, (r_me + k) % 8)

    def seq_peer(k):
        return ((s_me + k) % 16, r_me)

    def remote(src, dst, ssem, rsem, to):
        return pltpu.make_async_remote_copy(src, dst, ssem, rsem, device_id=to, device_id_type=MESH)

    own_rows = pl.ds(pl.multiple_of(r_me * 96, 96), 96)

    def all_sent(ref, sem):
        remote(ref, ref, sem, sem, twin).wait_send()

    def all_here(ref, sem):
        remote(ref, ref, sem, sem, twin).wait_recv()

    loads = [pltpu.make_async_copy(src, dst, lsem.at[i]) for i, (src, dst) in enumerate((
        (pair_hbm, pair_ref), (own_hbm.at[pl.ds(8 * y, 8)], rows_s.at[:, own_rows]), (rw_hbm, rw_ref), (cw_hbm, cw_ref),
        (own_hbm, own_ref)))]
    for load in loads:
        load.start()
    barrier = pltpu.get_barrier_semaphore()
    for k in range(1, 8):
        pl.semaphore_signal(barrier, inc=1, device_id=res_peer(k), device_id_type=MESH)
    for k in range(1, 16):
        pl.semaphore_signal(barrier, inc=1, device_id=seq_peer(k), device_id_type=MESH)
    rsend_ref[...] = jnp.zeros_like(rsend_ref)
    csend_ref[...] = jnp.zeros_like(csend_ref)
    live = ((flags_ref[...] * amino_ref[...]).astype(F32) - 1.0) * (1e9 * LOG2E)
    for b in range(4):
        rsend_ref[b, :, :96] = live[8 * b:8 * b + 8]
    lines = [flags_ref[8 * b + i:8 * b + i + 1, :] for i in range(8) for b in range(4)]
    seen = jnp.concatenate(lines, axis=0)
    seen = jnp.concatenate([(seen.astype(F32) - 1.0) * (1e9 * LOG2E), jnp.zeros((32, 32), F32)], axis=1)
    seen = jnp.transpose(seen)
    for a in range(16):
        csend_ref[a, :6, :32] = seen[6 * a:6 * a + 6]
    pl.semaphore_wait(barrier, 22)

    ALONG = ((along_x, along_y), (along_y, along_x))
    PLACE = ((x, y), (y, x))

    def region(p, phase, last=None):
        a, b = PLACE[p]
        if phase == 0:
            return buf.at[p, a, b, zhi, c]
        if phase == 1:
            return buf.at[p, a, b, :, c]
        return buf.at[p, :, (b if last is None else last), :, c]

    def ring(p, phase, d):
        at = region(p, phase)
        to = far if phase == 0 else ALONG[p][phase - 1](d)
        return remote(at, at, gsend.at[p, phase, d - 1], grecv.at[p, phase, d - 1], to)

    def pair(p, d):
        at = region(p, 2, (PLACE[p][1] - d) % 4)
        return remote(at, at, psend.at[p, d], precv.at[p, d], twin)

    def steps(phase):
        return (1,) if phase == 0 else (1, 3, 2)

    def start_rings(phase):
        for p in range(2):
            for d in steps(phase):
                ring(p, phase, d).start()

    def end_rings(phase):
        for p in range(2):
            for d in steps(phase):
                ring(p, phase, d).wait_recv()

    def y_copy(half, d):
        return remote(own_hbm.at[pl.ds((y + d) % 4 * 8 + 4 * half, 4)], rows_s.at[pl.ds(4 * half, 4), own_rows],
                      ysend.at[half, d], yrecv.at[half, d], along_y(d))

    def z_copy(half, d):
        at = rows_s.at[pl.ds(4 * half, 4), pl.ds(pl.multiple_of(((y - d) % 4 * 2 + zlo) * 96, 96), 96)]
        src = own_hbm.at[pl.ds(y * 8 + 4 * half, 4)] if d == 0 else at
        return remote(src, at, zsend.at[half, d], zrecv.at[half, d], near)

    def row_flags(k):
        return remote(rsend_ref.at[(r_me + k) % 8 // 2], rmask_s.at[r_me], rmsend, rmrecv, res_peer(k))

    def col_flags(k):
        return remote(csend_ref.at[(s_me + k) % 16], cmask_s.at[s_me], cmsend, cmrecv, seq_peer(k))

    z_copy(0, 0).start()
    for d in (1, 3, 2):
        y_copy(0, d).start()
    for k in range(1, 8):
        row_flags(k).start()

    loads[0].wait()
    pw = jnp.transpose(pw_ref[...].astype(F32)).astype(BF)
    flat = nt(pw, norm(pair_ref[...].reshape(4608, 128), pgain_ref[...]))
    for i in range(96):
        turn_s[i * 8:(i + 1) * 8, :48] = flat[:, i * 48:(i + 1) * 48]
    for p in range(2):
        a, b = PLACE[p]
        heads = [jnp.transpose(turn_s[pl.ds(4 * p + h, 96, stride=8), :])[:48] for h in range(4)]
        for m in range(3):
            both = jnp.concatenate([heads[m], heads[3][:, m * 32:(m + 1) * 32]], axis=1)
            buf[p, a, b, zhi, c, m * 48:(m + 1) * 48] = both.astype(BF)
    start_rings(0)

    rmask_s[r_me] = rsend_ref[y]
    cmask_s[s_me] = csend_ref[s_me]
    for load in loads[1:]:
        load.wait()
    for i, (w_ref, at) in enumerate(((rw_ref, 0), (cw_ref, 1))):
        wk_s[at] = jnp.zeros((CHAN, HEADS * 128), BF)
        for h in range(HEADS):
            wk_s[at, :, h * 128:h * 128 + WIDTH] = w_ref[1, :, h * WIDTH:(h + 1) * WIDTH]
        for j, m in enumerate((0, 2, 3)):
            wt_s[at, j] = jnp.transpose(w_ref[m].astype(F32)).astype(BF)
    one = lax.broadcasted_iota(jnp.int32, (QROWS - WIDTH, 3072), 0) == 0
    ones = jnp.where(one, 1.0, 0.0).astype(BF)
    for h in range(HEADS):
        q_s[h, WIDTH:, :] = ones
        v_s[h, WIDTH:, :] = jnp.ones((16, 6144), BF)
    for d in (1, 3, 2):
        y_copy(0, d).wait_recv()
        z_copy(0, d).start()
    for d in (1, 3, 2):
        y_copy(1, d).start()
    end_rings(0)
    start_rings(1)
    z_copy(1, 0).start()
    spot = lax.broadcasted_iota(jnp.int32, (512, 512), 0)
    line = spot % 32
    spot = line % 8 // 2 * 128 + spot // 32 * 8 + line % 2 * 4 + line // 8
    perm_s[...] = jnp.where(lax.broadcasted_iota(jnp.int32, (512, 512), 1) == spot, 1.0, 0.0).astype(BF)
    end_rings(1)
    start_rings(2)
    for p in range(2):
        pair(p, 0).start()
    for k in range(1, 16):
        col_flags(k).start()
    all_here(rmask_s.at[pl.ds(0, 7)], rmrecv)
    for d in range(4):
        z_copy(0, d).wait_recv()
    rtab = jnp.transpose(jnp.concatenate([rmask_s[b][:, :96] for b in range(8)], axis=1))

    def own_queries(ref):
        return jnp.concatenate([ref[pl.ds(pl.multiple_of((2 * b + zlo) * 96, 96), 96)] for b in range(4)], axis=0)

    def row_project(s, _):
        project(rows_s[s], rgain_ref[...], pick(rtab, s), wk_s.at[0], wt_s.at[0],
                [(0, 768, pl.multiple_of(s * 768, 256))], [(0, 384, pl.multiple_of(s * 384, 128))], own_queries,
                xn_s, k_s, q_s, v_s, g_s)
        return 0

    lax.fori_loop(0, 4, row_project, 0)

    for d in (1, 3, 2):
        for p in range(2):
            ring(p, 2, d).wait_recv()
            pair(p, d).start()
    for p in range(2):
        for d in range(4):
            pair(p, d).wait_recv()

    def scaled(b):
        return b.astype(F32) * LOG2E

    def assemble(s, _):
        at = pl.ds(pl.multiple_of(s * 48, 16), 48)
        for p in range(2):
            got = []
            for b in range(4):
                one, two = (s // 4, b) if p == 0 else (b, s // 4)
                got.append(buf[p, one, two, (s // 2) % 2, s % 2])
            for m in range(3):
                bias_s[4 * p + m, at, :] = scaled(jnp.concatenate([g[m * 48:(m + 1) * 48, :96] for g in got], axis=1))
            bias_s[4 * p + 3, at, :] = scaled(jnp.concatenate(
                [g[m * 48:(m + 1) * 48, 96:] for g in got for m in range(3)], axis=1))
        return 0

    lax.fori_loop(0, 16, assemble, 0)

    def back_copy(s, d):
        at = pl.ds(pl.multiple_of(s * 384 + (y + d) % 4 * 96, 96), 96)
        return remote(done_s.at[at], inc_ref.at[8 * y + s], bsend.at[s], brecv.at[s], along_y(d))

    def col_copy(s, k):
        return remote(out_s.at[s, (s_me + k) % 16], col_s.at[s_me, s], csend.at[s], crecv.at[s], seq_peer(k))

    def owner(s):
        for u in range(2):
            all_here(done_s.at[pl.ds(0, 288)], brecv.at[2 * s + u])
        parts = []
        for p in range(8):
            line = p % 4 * 8 + 2 * s + p // 4
            parts.append(own_ref[line].astype(F32) + inc_ref[line].astype(F32))
        both = jnp.swapaxes(jnp.stack(parts), 0, 1)
        out_s[s] = both.reshape(16, 48, CHAN).astype(BF)
        for k in range(1, 16):
            col_copy(s, k).start()
        col_s[s_me, s] = out_s[s, s_me]

    def row_step(s, _):
        lo = pl.multiple_of(s * 384, 128)
        attend(pl.multiple_of(s * 768, 256), 768, lo, 384, bias_s, k_s, q_s, v_s, g_s, o_s)
        done_s[pl.ds(lo, 384)] = tn(o_s[:, pl.ds(lo, 384)], ro_ref[...]).astype(BF)
        for d in (1, 3, 2):
            back_copy(s, d).start()
        inc_ref[8 * y + s] = done_s[pl.ds(pl.multiple_of(s * 384 + y * 96, 96), 96)]

        @pl.when(s == 0)
        def _():
            for d in (1, 3, 2):
                y_copy(1, d).wait_recv()
                z_copy(1, d).start()

        @pl.when(s == 3)
        def _():
            for d in range(4):
                z_copy(1, d).wait_recv()
            lax.fori_loop(4, 8, row_project, 0)

        @pl.when((s % 2 == 0) & (s > 0))
        def _():
            owner(s // 2 - 1)
        return 0

    lax.fori_loop(0, 8, row_step, 0)

    keep = pltpu.make_async_copy(inc_ref, inc_hbm, lsem.at[0])
    all_here(cmask_s.at[pl.ds(0, 15)], cmrecv)
    for a in range(16):
        turned = jnp.transpose(cmask_s[a])
        for s in range(4):
            ctab_s[s, a * 8:(a + 1) * 8, :8] = turned[s * 8:(s + 1) * 8]

    def col_project(s, _):
        all_here(out_s.at[s, pl.ds(0, 15)], crecv.at[s])
        six = col_s[:, s].astype(F32).reshape(16, 6, 8, CHAN)
        six = jnp.concatenate([six[:, r].reshape(128, CHAN) for r in range(6)], axis=0)
        tab = ctab_s[s]
        flag = jnp.concatenate([tab[:, r:r + 1] for r in range(6)], axis=0)
        spots = [(r * 128, 128, pl.multiple_of(r * 512 + s * 128, 128)) for r in range(6)]
        project(six, cgain_ref[...], flag, wk_s.at[1], wt_s.at[1],
                spots, spots, lambda ref: ref[...], xn_s, k_s, q_s, v_s, g_s)
        return 0

    lax.fori_loop(0, 2, col_project, 0)
    owner(3)
    keep.start()
    lax.fori_loop(2, 4, col_project, 0)

    def free(s, _):
        all_sent(done_s.at[pl.ds(0, 288)], bsend.at[s])
        return 0

    lax.fori_loop(0, 8, free, 0)

    def end_copy(r, k):
        to = (s_me + k) % 16
        at = pl.ds(pl.multiple_of(r * 512 + to * 32, 32), 32)
        return remote(done_s.at[at], fin_hbm.at[s_me, r], esend.at[r], erecv.at[r], seq_peer(k))

    def own_end(r):
        at = pl.ds(pl.multiple_of(r * 512 + s_me * 32, 32), 32)
        return pltpu.make_async_copy(done_s.at[at], fin_hbm.at[s_me, r], tsem.at[r])

    def col_step(r, _):
        lo = pl.multiple_of(r * 512, 512)
        attend(lo, 512, lo, 512, None, k_s, q_s, v_s, g_s, o_s)
        y = tn(o_s[:, pl.ds(lo, 512)], co_ref[...])
        done_s[pl.ds(lo, 512)] = nn(perm_s[...], y.astype(BF)).astype(BF)
        for k in range(1, 16):
            end_copy(r, k).start()
        own_end(r).start()
        return 0

    lax.fori_loop(0, 6, col_step, 0)

    all_sent(rmask_s.at[pl.ds(0, 7)], rmsend)
    all_sent(cmask_s.at[pl.ds(0, 15)], cmsend)
    for half in range(2):
        for d in range(1, 4):
            y_copy(half, d).wait_send()
        for d in range(4):
            z_copy(half, d).wait_send()
    for p in range(2):
        for phase in range(3):
            for d in steps(phase):
                ring(p, phase, d).wait_send()
        for d in range(4):
            pair(p, d).wait_send()

    def drain_cols(s, _):
        all_sent(out_s.at[s, pl.ds(0, 15)], csend.at[s])
        return 0

    lax.fori_loop(0, 4, drain_cols, 0)

    def drain(r, _):
        all_sent(done_s.at[pl.ds(0, 480)], esend.at[r])
        all_here(done_s.at[pl.ds(0, 480)], erecv.at[r])
        own_end(r).wait()
        return 0

    lax.fori_loop(0, 6, drain, 0)
    keep.wait()


def call(pair, pgain, pw, own, flags, amino, rgain, rw, ro, cgain, cw, co):
    args = (pair, pgain, pw, own, flags, amino, rgain, rw, ro, cgain, cw, co)
    dma = pltpu.SemaphoreType.DMA
    vmem = pl.BlockSpec(memory_space=pltpu.VMEM)
    hbm = pl.BlockSpec(memory_space=pl.ANY)
    return pl.pallas_call(
        kernel,
        out_shape=(jax.ShapeDtypeStruct((32, 96, CHAN), BF), jax.ShapeDtypeStruct((16, 6, 32, CHAN), BF)),
        in_specs=[hbm if i in (0, 3, 7, 10) else vmem for i in range(len(args))],
        out_specs=(hbm, hbm),
        scratch_shapes=[
            pltpu.VMEM((96, 48, 128), BF),
            pltpu.VMEM((32, 96, CHAN), BF),
            pltpu.VMEM((4, CHAN, CHAN), BF),
            pltpu.VMEM((4, CHAN, CHAN), BF),
            pltpu.VMEM((32, 96, CHAN), BF),
            pltpu.VMEM((512, 512), BF),
            pltpu.VMEM((2, 4, 4, 2, 2, 144, 128), BF),
            pltpu.VMEM((HEADS, 768, 384), F32),
            pltpu.VMEM((768, 128), F32),
            pltpu.VMEM((8, 8, 128), F32),
            pltpu.VMEM((16, 8, 128), F32),
            pltpu.VMEM((8, 768, CHAN), BF),
            pltpu.VMEM((8, 8, 128), F32),
            pltpu.VMEM((16, 8, 128), F32),
            pltpu.VMEM((16, 4, 48, CHAN), BF),
            pltpu.VMEM((4, 16, 48, CHAN), BF),
            pltpu.VMEM((3072, CHAN), BF),
            pltpu.VMEM((4, 128, 128), F32),
            pltpu.VMEM((768, CHAN), BF),
            pltpu.VMEM((6144, HEADS * 128), BF),
            pltpu.VMEM((HEADS, QROWS, 3072), BF),
            pltpu.VMEM((HEADS, WIDTH + 16, 6144), BF),
            pltpu.VMEM((CHAN, 3072), BF),
            pltpu.VMEM((CHAN, 3072), BF),
            pltpu.VMEM((2, CHAN, HEADS * 128), BF),
            pltpu.VMEM((2, 3, CHAN, CHAN), BF),
            dma((2, 3, 3)), dma((2, 3, 3)), dma((2, 4)), dma((2, 4)), dma((2, 4)), dma((2, 4)), dma((2, 4)), dma((2, 4)),
            dma((8,)), dma((8,)), dma((4,)), dma((4,)), dma((6,)), dma((6,)),
            dma(()), dma(()), dma(()), dma(()), dma((5,)), dma((6,)),
        ],
        compiler_params=pltpu.CompilerParams(collective_id=1, has_side_effects=True, vmem_limit_bytes=VLIM),
    )(*args)


def per_device(x, flags, amino, pair, pair_gain, pair_w, row_gain, row_w, row_o, col_gain, col_w, col_o):
    inc, fin = call(pair, pair_gain.reshape(1, -1), pair_w, x, flags, amino.reshape(1, -1),
                    row_gain.reshape(1, CHAN), row_w, row_o, col_gain.reshape(1, CHAN), col_w, col_o)
    upd = jnp.transpose(fin.reshape(96, 32, CHAN), (1, 0, 2))
    return inc, upd


def solution(mesh):
    ins = (P("seq", "res", None), P("seq", "res"), P("res"), P("res", "seq", None)) + (P(),) * 8
    outs = (P("seq", "res", None), P("seq", "res", None))
    return jax.shard_map(per_device, mesh=mesh, in_specs=ins, out_specs=outs, check_vma=False)
```

time: 721 us -> 140 us (0.19)
  waiting for transfers between devices: 398 us -> 0 us
  Pallas kernels: 0 us -> 133 us
  matrix products: 118 us -> 0 us
  local copies, waits for them, and re-layouts: 89.5 us -> 6.09 us
  other arithmetic: 60.5 us -> 0 us
  starting transfers between devices: 26.3 us -> 0 us
  between operations: 14.4 us -> 0.65 us
  blocking collectives: 11.3 us -> 0 us
    all_gather x1 -> x0, waiting for transfers between devices: 304 us -> none  [per_device(): lax.all_gather(bias_tile[None], ('seq', 'res'), axis=0, tiled=True)]
    pallas_call x0 -> x1, Pallas kernels: none -> 133 us  [call(): pl.pallas_call(kernel, out_shape=(jax.ShapeDtypeStruct((32, 96, CHAN), BF...]
    dot_general x25 -> x0, matrix products: 118 us -> none  [the longest x10 55.9 us: attend(): jnp.einsum('ihd,jhd->hij', asking_vectors, key_rows, preferred_element_ty...]
    all_to_all x5 -> x0, waiting for transfers between devices: 94.6 us -> none  [the longest x1 26.6 us: per_device(): lax.all_to_all(col_delta, 'seq', split_axis=0, concat_axis=1, tiled=True)]
    reduce_sum x16 -> x0, other arithmetic: 54.7 us -> none  [the longest x10 47 us: attend(): totals = jnp.sum(powers, axis=-1)]
    transpose x1 -> x0, local copies, waits for them, and re-layouts: 35.8 us -> none  [per_device(): jnp.transpose(stacked, (2, 1, 3, 0, 4))]
    all_to_all x5 -> x0, starting transfers between devices: 26.3 us -> none  [the longest x1 7.45 us: per_device(): lax.all_to_all(grouped, 'seq', split_axis=1, concat_axis=0, tiled=True)]
    reshape x2 -> x1, local copies, waits for them, and re-layouts: 21 us -> 3.55 us  [per_device(): upd = jnp.transpose(fin.reshape(96, 32, CHAN), (1, 0, 2))]
  transfers between devices with their start and end apart: 6 -> 0, of which waited for: 5 -> 0; matrix products, arithmetic and copies ran while one was open for 3% -> 0% of each run, Pallas kernels for 0% -> 0%
where the time goes in v1:
time: 140 us
  Pallas kernels  133 us (95%)
  local copies, waits for them, and re-layouts  6.09 us (4%)
    pallas_call x1, Pallas kernels, call(): pl.pallas_call(kernel, out_shape=(jax.ShapeDtypeStruct((32, 96, CHAN), BF...  133 us
    reshape x1, local copies, waits for them, and re-layouts, per_device(): upd = jnp.transpose(fin.reshape(96, 32, CHAN), (1, 0, 2))  3.55 us

profile of v1, /device:TPU:1, one launch (start us, length us, event | category | flops | bytes accessed | tf_op | source)
XLA Modules:
  0.0 140.0 jit_solution(5623779441591200797)
XLA Ops:
  0.6 1.4 copy.14.pw_ref
  2.0 133.3 %shard_map.131 = (bf16[32,96,256]{2,1,0:T(8,128)(2,1)}, bf16[16,6,32,256]{3,2,1,0:T(8,128)(2,1)}) custom-call(bf16[96,48,128]{2,1,0:T(8,128)(2,1)} %pair_hbm.1, f32[1,128]{1,0:T(1,128)} %bitcast.12, bf16[128,8]{1,0:T(8,128)(2,1)} %copy.14.pw_ref, bf16[32,96,256]{2,1,0:T(8,128)(2,1)} %own_hbm.1, s32[32,96]{1,0:T(8,128)} %flags_ref.1, s32[1,96]{1,0:T(1,128)} %bitcast.13, ...), custom_call_target="tpu_custom_call" | custom-call | tf_op jit(solution)/shard_map/pallas_call | solution.py:431
  135.3 0.0 copy-start
  135.3 3.5 %copy.17 = bf16[96,32,256]{2,0,1:T(8,128)(2,1)} copy(bf16[96,32,256]{2,1,0:T(8,128)(2,1)} %bitcast.9) | data formatting | bytes 3145728 | tf_op jit(solution)/shard_map/reshape | solution.py:474
  138.9 0.0 copy-done
  138.9 1.1 copy.19
Async XLA Ops:
  135.3 3.6 %copy-start = (bf16[32,96,256]{2,1,0:T(8,128)(2,1)S(1)}, bf16[32,96,256]{2,1,0:T(8,128)(2,1)}, u32[]{:S(2)}) copy-start(bf16[32,96,256]{2,1,0:T(8,128)(2,1)} %get-tuple-element.8) | copy-start | bytes 4718596
